TPU v7x, 32 devices: a whole 2x2x4 slice. The times are simulated.
32 devices in a mesh: seq: 8 (over y, x, core), head: 4 (over z).
Axes of the slice: x: 2, y: 2, z: 4, core: 2. Of those that a mesh axis runs over, the one named last changes fastest.
Arguments:
- query_rows: bfloat16 [4096, 2048], P('seq', 'head'), may hold values from -18 to 18
- key_rows: bfloat16 [4096, 2048], P('seq', 'head'), may hold values from -18 to 18
- value_rows: bfloat16 [4096, 2048], P('seq', 'head'), may hold values from -6 to 6
- out_grad: bfloat16 [4096, 4096], P('seq', 'head'), may hold values from -6 to 6
- out_weight: bfloat16 [2048, 4096], P('head', 'seq'), may hold values from -0.09375 to 0.09375
Outputs:
- attended: bfloat16 [4096, 2048], P('seq', 'head')
- query_grad: bfloat16 [4096, 2048], P('seq', 'head')
- key_grad: bfloat16 [4096, 2048], P('seq', 'head')
- value_grad: bfloat16 [4096, 2048], P('seq', 'head')
All inputs are finite; a program needn't handle non-finite values.
Results may differ from a plain program's by a relative error of at most 0.0067.
Values may be sent and summed in bfloat16 or wider, within the bound.
A program may use at most 64 MiB of HBM per device.

v0:
```python
import jax
import jax.numpy as jnp
from jax import lax
from jax.sharding import PartitionSpec as P

DH = 128
BLOCK = 128


SENTINEL = -1e30


def part_forward(queries, keys_part, values_part, visible, scaling, layout_forms):
    query_form, key_form, score_form, row_order, score_order = layout_forms
    scores = (
        jnp.einsum(
            query_form + "," + key_form + "->" + score_form,
            queries,
            keys_part,
            preferred_element_type=jnp.float32,
        )
        * scaling
    )
    row_max = jnp.max(jnp.where(visible, scores, SENTINEL), axis=-1)
    weights = jnp.where(visible, jnp.exp(scores - row_max[..., None]), 0.0)
    row_sum = jnp.sum(weights, axis=-1)
    partial_out = jnp.einsum(
        score_form + "," + key_form + "->" + query_form,
        weights.astype(jnp.bfloat16),
        values_part,
        preferred_element_type=jnp.float32,
    )
    return (
        scores,
        jnp.transpose(row_max, row_order),
        jnp.transpose(row_sum, row_order),
        partial_out,
    )


def part_backward(
    scores,
    visible,
    lse_rows,
    delta_rows,
    queries,
    keys_part,
    values_part,
    grad_part,
    scaling,
    layout_forms,
):
    query_form, key_form, score_form, row_order, score_order = layout_forms
    probs = jnp.where(
        visible, jnp.exp(scores - jnp.transpose(lse_rows, score_order)[..., None]), 0.0
    )
    value_part_grad = jnp.einsum(
        score_form + "," + query_form + "->" + key_form,
        probs.astype(jnp.bfloat16),
        grad_part,
        preferred_element_type=jnp.float32,
    )
    dprob = jnp.einsum(
        query_form + "," + key_form + "->" + score_form,
        grad_part,
        values_part,
        preferred_element_type=jnp.float32,
    )
    dscore = (probs * (dprob - jnp.transpose(delta_rows, score_order)[..., None])).astype(
        jnp.bfloat16
    )
    query_part_grad = (
        jnp.einsum(
            score_form + "," + key_form + "->" + query_form,
            dscore,
            keys_part,
            preferred_element_type=jnp.float32,
        )
        * scaling
    )
    key_part_grad = (
        jnp.einsum(
            score_form + "," + query_form + "->" + key_form,
            dscore,
            queries,
            preferred_element_type=jnp.float32,
        )
        * scaling
    )
    return (query_part_grad, key_part_grad, value_part_grad)


def combine_stats(max_band, sum_band, dot_band, max_strided, sum_strided, dot_strided):
    top = jnp.maximum(max_band, max_strided)
    band_factor = jnp.exp(max_band - top)
    strided_factor = jnp.exp(max_strided - top)
    total = band_factor * sum_band + strided_factor * sum_strided
    delta = (band_factor * dot_band + strided_factor * dot_strided) / total
    return (band_factor, strided_factor, total, top + jnp.log(total), delta)


def local(query_rows, key_rows, value_rows, out_grad, out_weight):
    tokens_here, width_here = query_rows.shape
    heads_here = width_here // DH
    groups = lax.axis_size("seq")
    residues = tokens_here // groups
    blocks_here = tokens_here // BLOCK
    scaling = DH ** (-0.5)
    band_forms = ("bihd", "bjhd", "bhij", (0, 2, 1), (0, 2, 1))
    strided_forms = ("ishd", "jshd", "shij", (2, 0, 1), (1, 2, 0))
    band_rows = lax.broadcasted_iota(jnp.int32, (BLOCK, BLOCK), 0)
    band_cols = lax.broadcasted_iota(jnp.int32, (BLOCK, BLOCK), 1)
    band_visible = band_cols <= band_rows
    far_rows = lax.broadcasted_iota(jnp.int32, (groups, groups), 0)
    far_cols = lax.broadcasted_iota(jnp.int32, (groups, groups), 1)
    strided_visible = far_cols < far_rows

    def band_view(values):
        return values.reshape(blocks_here, BLOCK, heads_here, DH)

    def group_view(values):
        return values.reshape(groups, residues, width_here)

    def strided_view(values):
        return values.reshape(groups, residues, heads_here, DH)

    full_grad = lax.all_gather(out_grad, "head", axis=1, tiled=True)
    grad_rows = lax.dot_general(
        full_grad,
        lax.all_gather(out_weight, "seq", axis=1, tiled=True),
        (((1,), (1,)), ((), ())),
        preferred_element_type=jnp.float32,
    ).astype(jnp.bfloat16)
    strided_query, strided_key, strided_value, strided_grad = (
        lax.all_to_all(group_view(query_rows), "seq", split_axis=0, concat_axis=0, tiled=True),
        lax.all_to_all(group_view(key_rows), "seq", split_axis=0, concat_axis=0, tiled=True),
        lax.all_to_all(group_view(value_rows), "seq", split_axis=0, concat_axis=0, tiled=True),
        lax.all_to_all(group_view(grad_rows), "seq", split_axis=0, concat_axis=0, tiled=True),
    )
    query_band = band_view(query_rows)
    key_band = band_view(key_rows)
    value_band = band_view(value_rows)
    band_scores, max_band, sum_band, out_band = part_forward(
        query_band, key_band, value_band, band_visible, scaling, band_forms
    )
    max_band = max_band.reshape(tokens_here, heads_here)
    sum_band = sum_band.reshape(tokens_here, heads_here)
    out_band = out_band.reshape(tokens_here, heads_here, DH)
    grad_heads = grad_rows.reshape(tokens_here, heads_here, DH)
    dot_band = jnp.sum(grad_heads.astype(jnp.float32) * out_band, axis=-1)
    far_query = strided_view(strided_query)
    far_key = strided_view(strided_key)
    far_value = strided_view(strided_value)
    far_scores, max_far, sum_far, out_far = part_forward(
        far_query, far_key, far_value, strided_visible, scaling, strided_forms
    )
    max_band_split = max_band.reshape(groups, residues, heads_here)
    sum_band_split = sum_band.reshape(groups, residues, heads_here)
    dot_band_split = dot_band.reshape(groups, residues, heads_here)
    home_out, home_max, home_sum, band_max_far, band_sum_far, band_dot_far = (
        lax.all_to_all(out_far, "seq", split_axis=0, concat_axis=0, tiled=True),
        lax.all_to_all(max_far, "seq", split_axis=0, concat_axis=0, tiled=True),
        lax.all_to_all(sum_far, "seq", split_axis=0, concat_axis=0, tiled=True),
        lax.all_to_all(max_band_split, "seq", split_axis=0, concat_axis=0, tiled=True),
        lax.all_to_all(sum_band_split, "seq", split_axis=0, concat_axis=0, tiled=True),
        lax.all_to_all(dot_band_split, "seq", split_axis=0, concat_axis=0, tiled=True),
    )
    home_out = home_out.reshape(tokens_here, heads_here, DH)
    home_max = home_max.reshape(tokens_here, heads_here)
    home_sum = home_sum.reshape(tokens_here, heads_here)
    home_dot = jnp.sum(grad_heads.astype(jnp.float32) * home_out, axis=-1)
    band_factor, far_factor, total, lse_home, delta_home = combine_stats(
        max_band, sum_band, dot_band, home_max, home_sum, home_dot
    )
    attended = (
        ((band_factor[..., None] * out_band + far_factor[..., None] * home_out) / total[..., None])
        .astype(jnp.bfloat16)
        .reshape(tokens_here, width_here)
    )
    far_grad = strided_view(strided_grad)
    far_dot = jnp.sum(far_grad.astype(jnp.float32) * out_far, axis=-1)
    far_stats = combine_stats(band_max_far, band_sum_far, band_dot_far, max_far, sum_far, far_dot)
    band_grads = part_backward(
        band_scores,
        band_visible,
        lse_home.reshape(blocks_here, BLOCK, heads_here),
        delta_home.reshape(blocks_here, BLOCK, heads_here),
        query_band,
        key_band,
        value_band,
        band_view(grad_rows),
        scaling,
        band_forms,
    )
    far_grads = part_backward(
        far_scores,
        strided_visible,
        far_stats[3],
        far_stats[4],
        far_query,
        far_key,
        far_value,
        far_grad,
        scaling,
        strided_forms,
    )
    home_query, home_key, home_value = (
        lax.all_to_all(
            far_grads[0].astype(jnp.bfloat16).reshape(groups, residues, width_here),
            "seq",
            split_axis=0,
            concat_axis=0,
            tiled=True,
        ),
        lax.all_to_all(
            far_grads[1].astype(jnp.bfloat16).reshape(groups, residues, width_here),
            "seq",
            split_axis=0,
            concat_axis=0,
            tiled=True,
        ),
        lax.all_to_all(
            far_grads[2].astype(jnp.bfloat16).reshape(groups, residues, width_here),
            "seq",
            split_axis=0,
            concat_axis=0,
            tiled=True,
        ),
    )
    query_grad = (
        band_grads[0].reshape(tokens_here, width_here)
        + home_query.reshape(tokens_here, width_here).astype(jnp.float32)
    ).astype(jnp.bfloat16)
    key_grad = (
        band_grads[1].reshape(tokens_here, width_here)
        + home_key.reshape(tokens_here, width_here).astype(jnp.float32)
    ).astype(jnp.bfloat16)
    value_grad = (
        band_grads[2].reshape(tokens_here, width_here)
        + home_value.reshape(tokens_here, width_here).astype(jnp.float32)
    ).astype(jnp.bfloat16)
    return (attended, query_grad, key_grad, value_grad)


def solution(mesh):
    placed = (
        P("seq", "head"),
        P("seq", "head"),
        P("seq", "head"),
        P("seq", "head"),
        P("head", "seq"),
    )
    return jax.shard_map(
        local,
        mesh=mesh,
        in_specs=placed,
        out_specs=(P("seq", "head"), P("seq", "head"), P("seq", "head"), P("seq", "head")),
        check_vma=False,
    )
```

profile of v0, /device:TPU:0, one launch (start us, length us, event | category | flops | bytes accessed | tf_op | source)
XLA Modules:
  0.0 262.8 jit_solution(13802554996167261505)
XLA Ops:
  12.2 9.7 %all_to_all.65 = f32[8,1,256]{2,1,0:T(1,128)S(1)} all-to-all(f32[8,1,256]{2,1,0:T(1,128)S(1)} %reshape.211), channel_id=1, replica_groups=mesh['seq'=8,'head'=4] {'seq'}, dimensions={0} | all-to-all | bytes 16384 | tf_op jit(solution)/shard_map/all_to_all | solution.py:165
  21.8 12.1 %all_to_all.66 = bf16[8,64,512]{2,1,0:T(8,128)(2,1)S(1)} all-to-all(bf16[8,64,512]{2,1,0:T(8,128)(2,1)S(1)} %bitcast.161), channel_id=1, replica_groups=mesh['seq'=8,'head'=4] {'seq'}, dimensions={0} | all-to-all | bytes 1048576 | tf_op jit(solution)/shard_map/all_to_all | solution.py:135
  34.0 3.5 %all-to-all-start.1 = ((bf16[8,64,512]{2,1,0:T(8,128)(2,1)}), bf16[8,64,512]{2,1,0:T(8,128)(2,1)S(1)}, u32[]{:S(2)}, u32[]{:S(2)}) async-start(bf16[8,64,512]{2,1,0:T(8,128)(2,1)} %bitcast.4), calls=%async_computation.1 | async-start | bytes 1048576 | tf_op jit(solution)/shard_map/all_to_all | solution.py:136
  38.3 8.9 %all-to-all-done.1 = bf16[8,64,512]{2,1,0:T(8,128)(2,1)S(1)} async-done(((bf16[8,64,512]{2,1,0:T(8,128)(2,1)}), bf16[8,64,512]{2,1,0:T(8,128)(2,1)S(1)}, u32[]{:S(2)}, u32[]{:S(2)}) %all-to-all-start.1) | async-done | bytes 524320 | tf_op jit(solution)/shard_map/all_to_all | solution.py:136
  47.1 3.3 %all-to-all-start.6 = ((f32[8,1,256]{2,1,0:T(1,128)}), f32[8,1,256]{2,1,0:T(1,128)S(1)}, u32[]{:S(2)}, u32[]{:S(2)}) async-start(f32[8,1,256]{2,1,0:T(1,128)} %reshape.209), calls=%async_computation.6 | async-start | bytes 16384 | tf_op jit(solution)/shard_map/all_to_all | solution.py:164
  50.5 2.0 reshape.180
  52.8 2.4 all-to-all-done.6
  55.1 4.1 %all-to-all-start.3 = ((bf16[8,64,512]{2,1,0:T(8,128)(2,1)}), bf16[8,64,512]{2,1,0:T(8,128)(2,1)}, u32[]{:S(2)}, u32[]{:S(2)}) async-start(bf16[8,64,512]{2,1,0:T(8,128)(2,1)} %bitcast.7), calls=%async_computation.3 | async-start | bytes 1048576 | tf_op jit(solution)/shard_map/all_to_all | solution.py:137
  62.2 6.8 %all-to-all-done.3 = bf16[8,64,512]{2,1,0:T(8,128)(2,1)} async-done(((bf16[8,64,512]{2,1,0:T(8,128)(2,1)}), bf16[8,64,512]{2,1,0:T(8,128)(2,1)}, u32[]{:S(2)}, u32[]{:S(2)}) %all-to-all-start.3) | async-done | bytes 524320 | tf_op jit(solution)/shard_map/all_to_all | solution.py:137
  69.0 3.3 %all-to-all-start.5 = ((f32[8,1,256]{2,1,0:T(1,128)}), f32[8,1,256]{2,1,0:T(1,128)S(1)}, u32[]{:S(2)}, u32[]{:S(2)}) async-start(f32[8,1,256]{2,1,0:T(1,128)} %reshape.205), calls=%async_computation.5 | async-start | bytes 16384 | tf_op jit(solution)/shard_map/all_to_all | solution.py:163
  72.4 20.7 %all-gather.3.cloned.1.call-done = bf16[512,4096]{1,0:T(8,128)(2,1)} async-done(((bf16[512,1024]{1,0:T(8,128)(2,1)}), bf16[512,4096]{1,0:T(8,128)(2,1)}) %all-gather.3.cloned.1.call-update) | async-done | bytes 4194320 | tf_op jit(solution)/shard_map/all_gather | solution.py:127
  93.1 37.9 %all-gather.5.cloned.1.call-done = bf16[512,4096]{1,0:T(8,128)(2,1)} async-done(((bf16[512,512]{1,0:T(8,128)(2,1)}), bf16[512,4096]{1,0:T(8,128)(2,1)}) %all-gather.5.cloned.1.call-update) | async-done | bytes 4194320 | tf_op jit(solution)/shard_map/all_gather | solution.py:130
  130.9 6.6 %convolution_convert_fusion.1 = bf16[512,512]{1,0:T(8,128)(2,1)} fusion(bf16[512,4096]{1,0:T(8,128)(2,1)} %all-gather.3.cloned.1.call-done, bf16[512,4096]{1,0:T(8,128)(2,1)} %all-gather.5.cloned.1.call-done), kind=kOutput, calls=%fused_computation.14 | convolution fusion | flops 2147745792 | bytes 8912896 | tf_op jit(solution)/shard_map/dot_general | solution.py:128
  139.1 3.3 %all-to-all-start.2 = ((f32[8,1,256]{2,1,0:T(1,128)}), f32[8,1,256]{2,1,0:T(1,128)S(1)}, u32[]{:S(2)}, u32[]{:S(2)}) async-start(f32[8,1,256]{2,1,0:T(1,128)} %reshape.203), calls=%async_computation.2 | async-start | bytes 16384 | tf_op jit(solution)/shard_map/all_to_all | solution.py:162
  144.0 3.0 %all-to-all-done.2 = f32[8,1,256]{2,1,0:T(1,128)S(1)} async-done(((f32[8,1,256]{2,1,0:T(1,128)}), f32[8,1,256]{2,1,0:T(1,128)S(1)}, u32[]{:S(2)}, u32[]{:S(2)}) %all-to-all-start.2) | async-done | bytes 8224 | tf_op jit(solution)/shard_map/all_to_all | solution.py:162
  147.0 7.7 %all_to_all.67 = f32[8,1,256]{2,1,0:T(1,128)} all-to-all(f32[8,1,256]{2,1,0:T(1,128)S(1)} %reshape.207), channel_id=1, replica_groups=mesh['seq'=8,'head'=4] {'seq'}, dimensions={0} | all-to-all | bytes 16384 | tf_op jit(solution)/shard_map/all_to_all | solution.py:166
  154.7 4.1 %all-to-all-start.8 = ((bf16[8,64,512]{2,1,0:T(8,128)(2,1)}), bf16[8,64,512]{2,1,0:T(8,128)(2,1)}, u32[]{:S(2)}, u32[]{:S(2)}) async-start(bf16[8,64,512]{2,1,0:T(8,128)(2,1)} %bitcast.16), calls=%async_computation.8 | async-start | bytes 1048576 | tf_op jit(solution)/shard_map/all_to_all | solution.py:138
  161.9 1.5 copy.145
  169.0 1.6 copy.143
  170.5 1.6 copy.152
  172.1 2.4 reshape.199
  178.9 1.7 fusion.27
  180.5 2.7 %multiply_reduce_fusion = (f32[8,64,4]{0,2,1:T(4,128)S(1)}, f32[8,64,4,128]{3,0,2,1:T(8,128)}) fusion(bf16[8,64,4,128]{3,2,1,0:T(4,128)(2,1)S(1)} %reshape.192, bf16[64,4,8,8]{3,2,1,0:T(8,128)(2,1)} %copy.145, bf16[8,64,4,128]{3,2,1,0:T(4,128)(2,1)S(1)} %reshape.183), kind=kOutput, calls=%fused_computation.31 | convolution fusion | flops 4978688 | bytes 2138112 | tf_op jit(solution)/shard_map/shij,jshd->ishd/dot_general | solution.py:27
  184.0 2.4 copy.183
  186.4 2.5 copy.147
  188.9 4.1 %all-to-all-start.4 = ((f32[8,64,4,128]{3,2,1,0:T(4,128)}), f32[8,64,4,128]{3,2,1,0:T(4,128)S(1)}, u32[]{:S(2)}, u32[]{:S(2)}) async-start(f32[8,64,4,128]{3,2,1,0:T(4,128)} %copy.147), calls=%async_computation.4 | async-start | bytes 2097152 | tf_op jit(solution)/shard_map/all_to_all | solution.py:161
  193.8 1.6 fusion.43
  195.4 2.5 copy.197
  197.9 1.5 fusion.8
  201.5 1.5 fusion.6
  204.1 2.1 reshape.196
  206.1 1.6 fusion.7
  208.9 4.3 %all-to-all-start.12 = ((bf16[8,64,512]{2,1,0:T(8,128)(2,1)}), bf16[8,64,512]{2,1,0:T(8,128)(2,1)}, u32[]{:S(2)}, u32[]{:S(2)}) async-start(bf16[8,64,512]{2,1,0:T(8,128)(2,1)} %reshape.198), calls=%async_computation.12 | async-start | bytes 1048576 | tf_op jit(solution)/shard_map/all_to_all | solution.py:222
  213.3 2.6 multiply_reduce_fusion.1
  217.0 1.5 convolution_bitcast_fusion.1
  218.4 2.5 copy.195
  222.2 2.7 %fusion.1 = f32[4,128,4,128]{1,3,2,0:T(8,128)} fusion(bf16[4,4,128,128]{2,3,1,0:T(8,128)(2,1)S(1)} %fusion.3, bf16[4,128,4,128]{3,2,1,0:T(4,128)(2,1)} %copy-done.7), kind=kOutput, calls=%fused_computation.6 | convolution fusion | flops 67371008 | bytes 2097152 | tf_op jit(solution)/shard_map/bhij,bihd->bjhd/dot_general | solution.py:82
  224.8 2.5 copy.189
  227.4 4.2 %all-to-all-start.11 = ((bf16[8,64,512]{2,1,0:T(8,128)(2,1)}), bf16[8,64,512]{2,1,0:T(8,128)(2,1)S(1)}, u32[]{:S(2)}, u32[]{:S(2)}) async-start(bf16[8,64,512]{2,1,0:T(8,128)(2,1)} %reshape.196), calls=%async_computation.11 | async-start | bytes 1048576 | tf_op jit(solution)/shard_map/all_to_all | solution.py:215
  231.6 2.4 fusion.2
  234.0 2.0 fusion.9
  236.0 5.3 %all-to-all-done.11 = bf16[8,64,512]{2,1,0:T(8,128)(2,1)S(1)} async-done(((bf16[8,64,512]{2,1,0:T(8,128)(2,1)}), bf16[8,64,512]{2,1,0:T(8,128)(2,1)S(1)}, u32[]{:S(2)}, u32[]{:S(2)}) %all-to-all-start.11) | async-done | bytes 524320 | tf_op jit(solution)/shard_map/all_to_all | solution.py:215
  241.3 3.5 %all-to-all-start.10 = ((bf16[8,64,512]{2,1,0:T(8,128)(2,1)}), bf16[8,64,512]{2,1,0:T(8,128)(2,1)S(1)}, u32[]{:S(2)}, u32[]{:S(2)}) async-start(bf16[8,64,512]{2,1,0:T(8,128)(2,1)} %reshape.194), calls=%async_computation.10 | async-start | bytes 1048576 | tf_op jit(solution)/shard_map/all_to_all | solution.py:208
  244.8 2.2 fusion.10
  247.0 1.6 copy.168
  249.2 1.6 mul.120
  250.8 1.6 div.18
  252.4 2.6 fusion.12
  (117 shorter events, 34.5 us)
Async XLA Ops:
  7.2 14.7 %copy-start.4 = (bf16[512,512]{1,0:T(8,128)(2,1)S(1)}, bf16[512,512]{1,0:T(8,128)(2,1)}, u32[]{:S(2)}) copy-start(bf16[512,512]{1,0:T(8,128)(2,1)} %param.5) | copy-start | bytes 1572868
  7.2 85.9 %all-gather.3.cloned.1.call-start = ((), (), s32[]{:S(2)}) async-start(), calls=%async_computation.13 | async-start | bytes 5242880 | tf_op jit(solution)/shard_map/all_gather | solution.py:127
  7.9 123.0 %all-gather.5.cloned.1.call-start = ((), (), s32[]{:S(2)}) async-start(), calls=%async_computation.14 | async-start | bytes 4718592 | tf_op jit(solution)/shard_map/all_gather | solution.py:130
  9.8 24.1 %copy-start.7 = (bf16[4,128,4,128]{3,2,1,0:T(4,128)(2,1)}, bf16[4,128,4,128]{3,2,1,0:T(4,128)(2,1)S(1)}, u32[]{:S(2)}) copy-start(bf16[4,128,4,128]{3,2,1,0:T(4,128)(2,1)S(1)} %reshape.172) | copy-start | bytes 1572868
  11.2 39.3 %copy-start.5 = (bf16[4,128,4,128]{3,2,1,0:T(4,128)(2,1)}, bf16[4,128,4,128]{3,2,1,0:T(4,128)(2,1)S(1)}, u32[]{:S(2)}) copy-start(bf16[4,128,4,128]{3,2,1,0:T(4,128)(2,1)S(1)} %reshape.173) | copy-start | bytes 1572868
  11.7 155.7 %copy-start.11 = (f32[4,4,128]{2,1,0:T(4,128)}, f32[4,4,128]{2,1,0:T(4,128)S(1)}, u32[]{:S(2)}) copy-start(f32[4,4,128]{2,1,0:T(4,128)S(1)} %get-tuple-element.15) | copy-start | bytes 24580
  12.0 155.5 %copy-start.14 = (f32[4,4,128]{2,1,0:T(4,128)}, f32[4,4,128]{2,1,0:T(4,128)S(1)}, u32[]{:S(2)}) copy-start(f32[4,4,128]{2,1,0:T(4,128)S(1)} %fusion.14) | copy-start | bytes 24580
  34.0 13.2 %all-to-all-start.1 = ((bf16[8,64,512]{2,1,0:T(8,128)(2,1)}), bf16[8,64,512]{2,1,0:T(8,128)(2,1)S(1)}, u32[]{:S(2)}, u32[]{:S(2)}) async-start(bf16[8,64,512]{2,1,0:T(8,128)(2,1)} %bitcast.4), calls=%async_computation.1 | async-start | bytes 1048576 | tf_op jit(solution)/shard_map/all_to_all | solution.py:136
  47.1 8.0 %all-to-all-start.6 = ((f32[8,1,256]{2,1,0:T(1,128)}), f32[8,1,256]{2,1,0:T(1,128)S(1)}, u32[]{:S(2)}, u32[]{:S(2)}) async-start(f32[8,1,256]{2,1,0:T(1,128)} %reshape.209), calls=%async_computation.6 | async-start | bytes 16384 | tf_op jit(solution)/shard_map/all_to_all | solution.py:164
  50.5 10.3 %copy-start.20 = (pred[8,8]{1,0:T(8,128)(4,1)}, pred[8,8]{1,0:T(8,128)(4,1)S(1)}, u32[]{:S(2)}) copy-start(pred[8,8]{1,0:T(8,128)(4,1)S(1)} %iota_compare_fusion.1) | copy-start | bytes 196
  52.6 85.0 %copy-start.1 = (bf16[8,64,4,128]{3,2,1,0:T(4,128)(2,1)}, bf16[8,64,4,128]{3,2,1,0:T(4,128)(2,1)S(1)}, u32[]{:S(2)}) copy-start(bf16[8,64,4,128]{3,2,1,0:T(4,128)(2,1)S(1)} %reshape.176) | copy-start | bytes 1572868
  52.8 84.8 %copy-start = (bf16[8,64,4,128]{3,2,1,0:T(4,128)(2,1)}, bf16[8,64,4,128]{3,2,1,0:T(4,128)(2,1)S(1)}, u32[]{:S(2)}) copy-start(bf16[8,64,4,128]{3,2,1,0:T(4,128)(2,1)S(1)} %reshape.178) | copy-start | bytes 1572868
  55.1 13.9 %all-to-all-start.3 = ((bf16[8,64,512]{2,1,0:T(8,128)(2,1)}), bf16[8,64,512]{2,1,0:T(8,128)(2,1)}, u32[]{:S(2)}, u32[]{:S(2)}) async-start(bf16[8,64,512]{2,1,0:T(8,128)(2,1)} %bitcast.7), calls=%async_computation.3 | async-start | bytes 1048576 | tf_op jit(solution)/shard_map/all_to_all | solution.py:137
  60.7 76.9 %copy-start.9 = (f32[64,4,8]{0,2,1:T(8,128)}, f32[64,4,8]{0,2,1:T(8,128)S(1)}, u32[]{:S(2)}) copy-start(f32[64,4,8]{0,2,1:T(8,128)S(1)} %select_reduce_fusion.1) | copy-start | bytes 24580
  60.8 76.7 %copy-start.13 = (f32[64,4,8]{0,2,1:T(8,128)}, f32[64,4,8]{0,2,1:T(8,128)S(1)}, u32[]{:S(2)}) copy-start(f32[64,4,8]{0,2,1:T(8,128)S(1)} %get-tuple-element.10) | copy-start | bytes 24580
  69.0 70.0 %all-to-all-start.5 = ((f32[8,1,256]{2,1,0:T(1,128)}), f32[8,1,256]{2,1,0:T(1,128)S(1)}, u32[]{:S(2)}, u32[]{:S(2)}) async-start(f32[8,1,256]{2,1,0:T(1,128)} %reshape.205), calls=%async_computation.5 | async-start | bytes 16384 | tf_op jit(solution)/shard_map/all_to_all | solution.py:163
  139.1 7.9 %all-to-all-start.2 = ((f32[8,1,256]{2,1,0:T(1,128)}), f32[8,1,256]{2,1,0:T(1,128)S(1)}, u32[]{:S(2)}, u32[]{:S(2)}) async-start(f32[8,1,256]{2,1,0:T(1,128)} %reshape.203), calls=%async_computation.2 | async-start | bytes 16384 | tf_op jit(solution)/shard_map/all_to_all | solution.py:162
  143.8 24.3 %copy-start.16 = (f32[4,128,4]{1,2,0:T(4,128)}, f32[4,128,4]{1,2,0:T(4,128)S(1)}, u32[]{:S(2)}) copy-start(f32[4,128,4]{1,2,0:T(4,128)S(1)} %get-tuple-element.17) | copy-start | bytes 24580
  154.7 22.9 %all-to-all-start.8 = ((bf16[8,64,512]{2,1,0:T(8,128)(2,1)}), bf16[8,64,512]{2,1,0:T(8,128)(2,1)}, u32[]{:S(2)}, u32[]{:S(2)}) async-start(bf16[8,64,512]{2,1,0:T(8,128)(2,1)} %bitcast.16), calls=%async_computation.8 | async-start | bytes 1048576 | tf_op jit(solution)/shard_map/all_to_all | solution.py:138
  188.9 20.1 %all-to-all-start.4 = ((f32[8,64,4,128]{3,2,1,0:T(4,128)}), f32[8,64,4,128]{3,2,1,0:T(4,128)S(1)}, u32[]{:S(2)}, u32[]{:S(2)}) async-start(f32[8,64,4,128]{3,2,1,0:T(4,128)} %copy.147), calls=%async_computation.4 | async-start | bytes 2097152 | tf_op jit(solution)/shard_map/all_to_all | solution.py:161
  195.4 5.3 %copy-start.10 = (bf16[64,4,8,8]{0,3,2,1:T(8,128)(2,1)S(1)}, bf16[64,4,8,8]{0,3,2,1:T(8,128)(2,1)}, u32[]{:S(2)}) copy-start(bf16[64,4,8,8]{0,3,2,1:T(8,128)(2,1)} %get-tuple-element.8) | copy-start | bytes 98308
  204.0 12.9 %copy-start.12 = (f32[4,4,128]{2,1,0:T(4,128)S(1)}, f32[4,4,128]{2,1,0:T(4,128)}, u32[]{:S(2)}) copy-start(f32[4,4,128]{2,1,0:T(4,128)} %copy-done.11) | copy-start | bytes 24580
  204.0 12.9 %copy-start.15 = (f32[4,4,128]{2,1,0:T(4,128)S(1)}, f32[4,4,128]{2,1,0:T(4,128)}, u32[]{:S(2)}) copy-start(f32[4,4,128]{2,1,0:T(4,128)} %copy-done.14) | copy-start | bytes 24580
  204.0 12.9 %copy-start.17 = (f32[4,128,4]{1,2,0:T(4,128)S(1)}, f32[4,128,4]{1,2,0:T(4,128)}, u32[]{:S(2)}) copy-start(f32[4,128,4]{1,2,0:T(4,128)} %copy-done.16) | copy-start | bytes 24580
  204.0 12.9 %copy-start.18 = (f32[4,128,4]{1,0,2:T(4,128)S(1)}, f32[4,128,4]{1,0,2:T(4,128)}, u32[]{:S(2)}) copy-start(f32[4,128,4]{1,0,2:T(4,128)} %reshape.188) | copy-start | bytes 24580
  204.0 12.9 %copy-start.19 = (f32[4,128,4]{1,0,2:T(4,128)S(1)}, f32[4,128,4]{1,0,2:T(4,128)}, u32[]{:S(2)}) copy-start(f32[4,128,4]{1,0,2:T(4,128)} %reshape.187) | copy-start | bytes 24580
  208.9 12.0 %copy-start.3 = (bf16[4,128,4,128]{3,2,1,0:T(4,128)(2,1)S(1)}, bf16[4,128,4,128]{3,2,1,0:T(4,128)(2,1)}, u32[]{:S(2)}) copy-start(bf16[4,128,4,128]{3,2,1,0:T(4,128)(2,1)} %reshape.180) | copy-start | bytes 1572868
  208.9 18.4 %all-to-all-start.12 = ((bf16[8,64,512]{2,1,0:T(8,128)(2,1)}), bf16[8,64,512]{2,1,0:T(8,128)(2,1)}, u32[]{:S(2)}, u32[]{:S(2)}) async-start(bf16[8,64,512]{2,1,0:T(8,128)(2,1)} %reshape.198), calls=%async_computation.12 | async-start | bytes 1048576 | tf_op jit(solution)/shard_map/all_to_all | solution.py:222
  221.4 0.8 copy-start.8
  222.1 9.4 %copy-start.6 = (bf16[4,128,4,128]{3,2,1,0:T(4,128)(2,1)S(1)}, bf16[4,128,4,128]{3,2,1,0:T(4,128)(2,1)}, u32[]{:S(2)}) copy-start(bf16[4,128,4,128]{3,2,1,0:T(4,128)(2,1)} %copy-done.5) | copy-start | bytes 1572868
  222.1 11.8 %copy-start.2 = (f32[4,128,4,128]{3,2,1,0:T(4,128)S(1)}, f32[4,128,4,128]{3,2,1,0:T(4,128)}, u32[]{:S(2)}) copy-start(f32[4,128,4,128]{3,2,1,0:T(4,128)} %copy.195) | copy-start | bytes 3145732
  227.4 13.9 %all-to-all-start.11 = ((bf16[8,64,512]{2,1,0:T(8,128)(2,1)}), bf16[8,64,512]{2,1,0:T(8,128)(2,1)S(1)}, u32[]{:S(2)}, u32[]{:S(2)}) async-start(bf16[8,64,512]{2,1,0:T(8,128)(2,1)} %reshape.196), calls=%async_computation.11 | async-start | bytes 1048576 | tf_op jit(solution)/shard_map/all_to_all | solution.py:215
  241.3 13.7 %all-to-all-start.10 = ((bf16[8,64,512]{2,1,0:T(8,128)(2,1)}), bf16[8,64,512]{2,1,0:T(8,128)(2,1)S(1)}, u32[]{:S(2)}, u32[]{:S(2)}) async-start(bf16[8,64,512]{2,1,0:T(8,128)(2,1)} %reshape.194), calls=%async_computation.10 | async-start | bytes 1048576 | tf_op jit(solution)/shard_map/all_to_all | solution.py:208
Sparse Core Ops, SparseCore 0:
  9.6 83.4 all-gather.2
  94.9 35.9 all-gather.4
where the time goes:
time: 265 us; the launch traced here: 263 us
  waiting for transfers between devices  86.3 us (33%)
  local copies, waits for them, and re-layouts  51.7 us (20%)
  starting transfers between devices  37.9 us (14%)
  blocking collectives  29.5 us (11%)
  matrix products  25.2 us (10%)
  other arithmetic  17.6 us (7%)
  between operations  14.5 us (5%)
    all_gather x1, waiting for transfers between devices, local(): lax.all_gather(out_weight, 'seq', axis=1, tiled=True)  37.9 us
    all_gather x1, waiting for transfers between devices, local(): full_grad = lax.all_gather(out_grad, 'head', axis=1, tiled=True)  20.7 us
    all_to_all x1, blocking collectives, local(): lax.all_to_all(group_view(query_rows), 'seq', split_axis=0, concat_axis=0...  12.1 us
    all_to_all x1, blocking collectives, local(): lax.all_to_all(sum_band_split, 'seq', split_axis=0, concat_axis=0, tiled=...  9.66 us
    all_to_all x1, waiting for transfers between devices, local(): lax.all_to_all(group_view(key_rows), 'seq', split_axis=0, concat_axis=0,...  8.89 us
    all_to_all x1, blocking collectives, local(): lax.all_to_all(dot_band_split, 'seq', split_axis=0, concat_axis=0, tiled=...  7.73 us
    all_to_all x1, waiting for transfers between devices, local(): lax.all_to_all(group_view(value_rows), 'seq', split_axis=0, concat_axis=0...  6.78 us
    dot_general x1, matrix products, local(): lax.dot_general(full_grad, lax.all_gather(out_weight, 'seq', axis=1, tile...  6.62 us
  transfers between devices with their start and end apart: 12, of which 7 were waited for; matrix products, arithmetic and copies ran while one was open for 31% of the time, Pallas kernels for 0%

commit v1 on v0

--- a/solution.py
+++ b/solution.py
@@ -1,4 +1,8 @@
+import functools
+
 import jax
+import jax.experimental.pallas as pl
+import jax.experimental.pallas.tpu as pltpu
 import jax.numpy as jnp
 from jax import lax
 from jax.sharding import PartitionSpec as P
@@ -242,6 +246,472 @@
     return (attended, query_grad, key_grad, value_grad)
 
 
+MESH = pl.DeviceIdType.MESH
+STAT = 128
+ROWS = 16
+
+
+def dot_nt(a, b):
+    return lax.dot_general(a, b, (((1,), (1,)), ((), ())), preferred_element_type=jnp.float32)
+
+
+def dot_nn(a, b):
+    return lax.dot_general(a, b, (((1,), (0,)), ((), ())), preferred_element_type=jnp.float32)
+
+
+def dot_tn(a, b):
+    return lax.dot_general(a, b, (((0,), (0,)), ((), ())), preferred_element_type=jnp.float32)
+
+
+def pack_stats(columns):
+    rows = columns[0].shape[0]
+    lane = lax.broadcasted_iota(jnp.int32, (rows, STAT), 1)
+    which = lane % 8
+    spread = jnp.zeros((rows, STAT), jnp.float32)
+    for index, column in enumerate(columns):
+        spread = jnp.where(which == index, column, spread)
+    first = spread.astype(jnp.bfloat16).astype(jnp.float32)
+    rest = spread - first
+    second = rest.astype(jnp.bfloat16).astype(jnp.float32)
+    third = rest - second
+    packed = jnp.where(lane < 8, first, jnp.where(lane < 16, second, jnp.where(lane < 24, third, 0.0)))
+    return packed.astype(jnp.bfloat16)
+
+
+def unpack_stat(packed, index):
+    lane = lax.broadcasted_iota(jnp.int32, packed.shape, 1)
+    return jnp.sum(jnp.where(lane % 8 == index, packed, 0.0), axis=1, keepdims=True)
+
+
+def fused_kernel(
+    groups, heads, chunks, planes,
+    q, k, v, og, w,
+    att_out, dq_out, dk_out, dv_out,
+    og_all, w_all, qf, kf, vf, g_home, gf, far_out, home_out, gr_send, gr_home,
+    out_band, att_full, lse_keep, s_band, s_far, band_grads,
+    z_send, z_recv, w_send, w_recv, qkv_send, qkv_recv, out_send, out_recv,
+    g_send, g_recv, gr_ssem, gr_rsem,
+):
+    s = lax.axis_index("seq")
+    h = lax.axis_index("head")
+    width = heads * DH
+    scaling = DH ** (-0.5)
+    blocks = groups // 2
+    block_rows = groups * ROWS
+    row = lax.broadcasted_iota(jnp.int32, (block_rows, block_rows), 0)
+    col = lax.broadcasted_iota(jnp.int32, (block_rows, block_rows), 1)
+    band_mask = col <= row
+    far_mask = (row % ROWS == col % ROWS) & (col // ROWS < row // ROWS)
+
+    def remote(src, dst, ssem, rsem, to):
+        return pltpu.make_async_remote_copy(
+            src_ref=src, dst_ref=dst, send_sem=ssem, recv_sem=rsem, device_id=to, device_id_type=MESH
+        )
+
+    core, x, y = s % 2, s // 2 % 2, s // 4
+
+    def other(o):
+        return (
+            (1 - y if o & 4 else y) * 4 + (1 - x if o & 2 else x) * 2 + (1 - core if o & 1 else core)
+        )
+
+    def peer(o):
+        return (other(o), h)
+
+    barrier = pltpu.get_barrier_semaphore()
+    for o in range(1, groups):
+        pl.semaphore_signal(barrier, inc=1, device_id=peer(o), device_id_type=MESH)
+    for z in range(planes):
+        @pl.when((h == z + 1) | (h == z - 1))
+        def _():
+            pl.semaphore_signal(barrier, inc=1, device_id=(s, z), device_id_type=MESH)
+    inner = (h > 0) & (h < planes - 1)
+
+    @pl.when(inner)
+    def _():
+        pl.semaphore_wait(barrier, groups + 1)
+
+    @pl.when(jnp.logical_not(inner))
+    def _():
+        pl.semaphore_wait(barrier, groups)
+
+    def z_copy(slot, c, direction):
+        mine = og_all.at[slot, c]
+        return remote(mine, mine, z_send.at[direction, slot, c], z_recv.at[slot, c],
+                      (s, h + (1 if direction == 0 else -1)))
+
+    def z_own(c, direction):
+        return remote(og.at[:, c], og_all.at[h, c], z_send.at[direction, h, c], z_recv.at[h, c],
+                      (s, h + (1 if direction == 0 else -1)))
+
+    def z_pass(slot, c):
+        @pl.when(h != slot)
+        def _():
+            z_copy(slot, c, 0).wait_recv()
+
+        @pl.when((h > slot) & (h < planes - 1))
+        def _():
+            z_copy(slot, c, 0).start()
+
+        @pl.when((h < slot) & (h > 0))
+        def _():
+            z_copy(slot, c, 1).start()
+
+    @pl.loop(0, chunks)
+    def _(c):
+        @pl.when(h < planes - 1)
+        def _():
+            z_own(c, 0).start()
+
+        @pl.when(h > 0)
+        def _():
+            z_own(c, 1).start()
+
+    half = w.shape[0] // 2
+    low, high = pl.ds(0, half), pl.ds(half, half)
+
+    def w_own(index, o):
+        return remote(w, w_all.at[s], w_send.at[index], w_recv.at[index], peer(o))
+
+    def w_part(index, source, rows, o):
+        ref = w_all.at[source, rows]
+        return remote(ref, ref, w_send.at[index], w_recv.at[index], peer(o))
+
+    w_first = [w_own(0, 2), w_own(1, 4), w_own(2, 1)]
+    for copy in w_first:
+        copy.start()
+
+    def qkv_copy(t, src, dst, o):
+        return remote(src.at[other(o)], dst.at[:, s], qkv_send.at[t, o], qkv_recv.at[t, o], peer(o))
+
+    triples = ((q, qf), (k, kf), (v, vf))
+    for o in (6, 2, 4, 7, 3, 5, 1):
+        for t, (src, dst) in enumerate(triples):
+            qkv_copy(t, src, dst, o).start()
+    for src, dst in triples:
+        dst[:, s] = src[s]
+    w_all[s] = w[...]
+
+    def forward_block(queries, keys_part, values_part, mask):
+        scores = dot_nt(queries, keys_part) * scaling
+        row_max = jnp.max(jnp.where(mask, scores, SENTINEL), axis=1, keepdims=True)
+        weights = jnp.where(mask, jnp.exp(scores - row_max), 0.0)
+        row_sum = jnp.maximum(jnp.sum(weights, axis=1, keepdims=True), 1.0)
+        partial = dot_nn(weights.astype(jnp.bfloat16), values_part) / row_sum
+        return scores, row_max + jnp.log(row_sum), partial
+
+    def columns(head):
+        return slice(head * DH, (head + 1) * DH)
+
+    def natural(ref, b):
+        return ref[pl.ds(2 * b, 2)].reshape(block_rows, ref.shape[-1])
+
+    def place(column, head, rows):
+        lane = lax.broadcasted_iota(jnp.int32, (rows, STAT), 1)
+        return jnp.where(lane == head, column, 0.0)
+
+    @pl.loop(0, blocks)
+    def _(b):
+        qb, kb, vb = natural(q, b), natural(k, b), natural(v, b)
+        kept = jnp.zeros((block_rows, STAT), jnp.float32)
+        for head in range(heads):
+            at = columns(head)
+            scores, lse, partial = forward_block(qb[:, at], kb[:, at], vb[:, at], band_mask)
+            s_band[b * heads + head] = scores
+            out_band[b, :, at] = partial
+            kept = kept + place(lse, head, block_rows)
+        lse_keep[pl.ds(2 * b, 2)] = kept.reshape(2, chunks, ROWS, STAT)
+
+    w_own(0, 2).wait_recv()
+    w_second = [w_part(3, other(2), low, 4), w_part(4, other(2), slice(None), 1)]
+    for copy in w_second:
+        copy.start()
+    w_own(1, 4).wait_recv()
+    w_third = [w_part(5, other(4), high, 2), w_part(6, other(4), slice(None), 1)]
+    for copy in w_third:
+        copy.start()
+
+    def z_near(c):
+        for slot in range(planes):
+            @pl.when((h == slot + 1) | (h == slot - 1))
+            def _():
+                z_pass(slot, c)
+
+    def z_far(c):
+        for distance in range(2, planes):
+            for slot in range(planes):
+                @pl.when((h == slot + distance) | (h == slot - distance))
+                def _():
+                    z_pass(slot, c)
+
+    @pl.loop(0, chunks)
+    def _(c):
+        z_near(c)
+
+    w_part(3, other(6), low, 4).wait_recv()
+    w_fourth = [w_part(7, other(6), low, 1)]
+    w_fourth[0].start()
+    w_part(5, other(6), high, 2).wait_recv()
+    w_fourth.append(w_part(8, other(6), high, 1))
+    w_fourth[1].start()
+
+    for o in range(1, groups):
+        for t, (src, dst) in enumerate(triples):
+            qkv_copy(t, src, dst, o).wait_recv()
+
+    def out_copy(c, o):
+        return remote(far_out.at[c, other(o)], home_out.at[s, c], out_send.at[c, o], out_recv.at[c, o], peer(o))
+
+    def out_arrived(c, o):
+        return remote(far_out.at[c, other(o)], home_out.at[other(o), c], out_send.at[c, o], out_recv.at[c, o], peer(o))
+
+    def chunk_of(ref, c):
+        return ref[c].reshape(block_rows, ref.shape[-1])
+
+    @pl.loop(0, chunks)
+    def _(c):
+        qb, kb, vb = chunk_of(qf, c), chunk_of(kf, c), chunk_of(vf, c)
+        stats = []
+        for head in range(heads):
+            at = columns(head)
+            scores, lse, partial = forward_block(qb[:, at], kb[:, at], vb[:, at], far_mask)
+            s_far[c * heads + head] = scores
+            far_out[c, :, :, at] = partial.astype(jnp.bfloat16).reshape(groups, ROWS, DH)
+            stats.append(lse)
+        far_out[c, :, :, width:] = pack_stats(stats).reshape(groups, ROWS, STAT)
+        for o in range(1, groups):
+            out_copy(c, o).start()
+        home_out[s, c] = far_out[c, s]
+
+    @pl.loop(0, chunks)
+    def _(c):
+        @pl.when(inner)
+        def _():
+            z_far(c)
+
+    w_own(2, 1).wait_recv()
+    w_part(4, other(3), slice(None), 1).wait_recv()
+    w_part(6, other(5), slice(None), 1).wait_recv()
+    w_part(7, other(7), low, 1).wait_recv()
+    w_part(8, other(7), high, 1).wait_recv()
+
+    @pl.loop(0, chunks)
+    def _(c):
+        for o in range(1, groups):
+            out_arrived(c, o).wait_recv()
+
+    @pl.loop(0, blocks)
+    def _(b):
+        message = natural(home_out, b)
+        packed = message[:, width:].astype(jnp.float32)
+        band = natural(lse_keep, b)
+        kept = jnp.zeros((block_rows, STAT), jnp.float32)
+        for head in range(heads):
+            at = columns(head)
+            lse_far = unpack_stat(packed, head)
+            lse_near = band[:, head:head + 1]
+            top = jnp.maximum(lse_far, lse_near)
+            near_factor = jnp.exp(lse_near - top)
+            far_factor = jnp.exp(lse_far - top)
+            total = near_factor + far_factor
+            combined = (near_factor * out_band[b, :, at] + far_factor * message[:, at].astype(jnp.float32)) / total
+            att_full[pl.ds(2 * b, 2), :, :, at] = combined.reshape(2, chunks, ROWS, DH)
+            att_out[pl.ds(2 * b, 2), :, :, at] = combined.astype(jnp.bfloat16).reshape(2, chunks, ROWS, DH)
+            kept = kept + place(top + jnp.log(total), head, block_rows)
+        lse_keep[pl.ds(2 * b, 2)] = kept.reshape(2, chunks, ROWS, STAT)
+
+    def g_copy(c, o):
+        return remote(g_home.at[other(o), c], gf.at[c, s], g_send.at[c, o], g_recv.at[c, o], peer(o))
+
+    def g_arrived(c, o):
+        return remote(g_home.at[other(o), c], gf.at[c, other(o)], g_send.at[c, o], g_recv.at[c, o], peer(o))
+
+    def gr_copy(c, o):
+        return remote(gr_send.at[c, other(o)], gr_home.at[s, c], gr_ssem.at[c, o], gr_rsem.at[c, o], peer(o))
+
+    def gr_arrived(c, o):
+        return remote(gr_send.at[c, other(o)], gr_home.at[other(o), c], gr_ssem.at[c, o], gr_rsem.at[c, o], peer(o))
+
+    @pl.loop(0, chunks)
+    def _(c):
+        og_all[h, c] = og[:, c]
+
+    def grad_chunk(c):
+        @pl.when(jnp.logical_not(inner))
+        def _():
+            z_far(c)
+        total = jnp.zeros((block_rows, width), jnp.float32)
+        depth = w.shape[1]
+        for source in range(groups):
+            per = og.shape[-1] // depth
+            left = og_all[source // per, c, :, :, (source % per) * depth:(source % per + 1) * depth]
+            total = total + dot_nt(left.reshape(block_rows, depth), w_all[source])
+        grad = total.astype(jnp.bfloat16)
+        g_home[:, c, :, :width] = grad.reshape(groups, ROWS, width)
+        grad = grad.astype(jnp.float32)
+        attended = att_full[:, c].reshape(block_rows, width)
+        kept = lse_keep[:, c].reshape(block_rows, STAT)
+        stats = [kept[:, head:head + 1] for head in range(heads)]
+        stats += [jnp.sum(grad[:, columns(head)] * attended[:, columns(head)], axis=1, keepdims=True) for head in range(heads)]
+        g_home[:, c, :, width:] = pack_stats(stats).reshape(groups, ROWS, STAT)
+        for o in range(1, groups):
+            g_copy(c, o).start()
+        gf[c, s] = g_home[s, c]
+
+    def backward_block(scores, mask, lse, delta, queries, keys_part, values_part, grad_part):
+        probs = jnp.where(mask, jnp.exp(scores - lse), 0.0)
+        value_part = dot_tn(probs.astype(jnp.bfloat16), grad_part)
+        dprob = dot_nt(grad_part, values_part)
+        dscore = (probs * (dprob - delta)).astype(jnp.bfloat16)
+        return dot_nn(dscore, keys_part) * scaling, dot_tn(dscore, queries) * scaling, value_part
+
+    def far_backward(c):
+        for o in range(1, groups):
+            g_arrived(c, o).wait_recv()
+        qb, kb, vb, message = chunk_of(qf, c), chunk_of(kf, c), chunk_of(vf, c), chunk_of(gf, c)
+        packed = message[:, width:].astype(jnp.float32)
+        for head in range(heads):
+            at = columns(head)
+            parts = backward_block(
+                s_far[c * heads + head], far_mask, unpack_stat(packed, head), unpack_stat(packed, heads + head),
+                qb[:, at], kb[:, at], vb[:, at], message[:, at],
+            )
+            for t, part in enumerate(parts):
+                gr_send[c, :, t, :, at] = part.astype(jnp.bfloat16).reshape(groups, ROWS, DH)
+        for o in range(1, groups):
+            gr_copy(c, o).start()
+        gr_home[s, c] = gr_send[c, s]
+
+    @pl.loop(0, chunks + 1)
+    def _(c):
+        @pl.when(c < chunks)
+        def _():
+            grad_chunk(c)
+
+        @pl.when(c > 0)
+        def _():
+            far_backward(c - 1)
+
+    @pl.loop(0, blocks)
+    def _(b):
+        qb, kb, vb, message = natural(q, b), natural(k, b), natural(v, b), natural(g_home, b)
+        packed = message[:, width:].astype(jnp.float32)
+        for head in range(heads):
+            at = columns(head)
+            parts = backward_block(
+                s_band[b * heads + head], band_mask, unpack_stat(packed, head), unpack_stat(packed, heads + head),
+                qb[:, at], kb[:, at], vb[:, at], message[:, at],
+            )
+            for t, part in enumerate(parts):
+                band_grads[t, b, :, at] = part
+
+    @pl.loop(0, chunks)
+    def _(c):
+        for o in range(1, groups):
+            gr_arrived(c, o).wait_recv()
+
+    @pl.loop(0, blocks)
+    def _(b):
+        for t, result in enumerate((dq_out, dk_out, dv_out)):
+            arrived = gr_home[pl.ds(2 * b, 2), :, t].reshape(block_rows, width).astype(jnp.float32)
+            result[pl.ds(2 * b, 2)] = (
+                (band_grads[t, b] + arrived).astype(jnp.bfloat16).reshape(2, chunks, ROWS, width)
+            )
+
+    for copy in w_first + w_second + w_third + w_fourth:
+        copy.wait_send()
+    for o in range(1, groups):
+        for t, (src, dst) in enumerate(triples):
+            qkv_copy(t, src, dst, o).wait_send()
+
+    @pl.loop(0, chunks)
+    def _(c):
+        for o in range(1, groups):
+            out_copy(c, o).wait_send()
+            g_copy(c, o).wait_send()
+            gr_copy(c, o).wait_send()
+
+        @pl.when(h < planes - 1)
+        def _():
+            z_own(c, 0).wait_send()
+
+        @pl.when(h > 0)
+        def _():
+            z_own(c, 1).wait_send()
+
+        for slot in range(planes):
+            @pl.when((h > slot) & (h < planes - 1))
+            def _():
+                z_copy(slot, c, 0).wait_send()
+
+            @pl.when((h < slot) & (h > 0))
+            def _():
+                z_copy(slot, c, 1).wait_send()
+
+
+def fused_local(query_rows, key_rows, value_rows, out_grad, out_weight):
+    tokens_here, width = query_rows.shape
+    heads = width // DH
+    groups = lax.axis_size("seq")
+    planes = lax.axis_size("head")
+    chunks = tokens_here // groups // ROWS
+    depth = out_grad.shape[1]
+    block_rows = groups * ROWS
+    blocks = tokens_here // block_rows
+
+    def split(values):
+        return values.reshape(groups, chunks, ROWS, values.shape[1])
+
+    half, full = jnp.bfloat16, jnp.float32
+    dma = pltpu.SemaphoreType.DMA
+    in_vmem = pl.BlockSpec(memory_space=pltpu.VMEM)
+    results = pl.pallas_call(
+        functools.partial(fused_kernel, groups, heads, chunks, planes),
+        out_shape=[jax.ShapeDtypeStruct((groups, chunks, ROWS, width), half)] * 4,
+        in_specs=[in_vmem] * 5,
+        out_specs=[in_vmem] * 4,
+        scratch_shapes=[
+            pltpu.VMEM((planes, chunks, groups, ROWS, depth), half),
+            pltpu.VMEM((groups,) + out_weight.shape, half),
+            pltpu.VMEM((chunks, groups, ROWS, width), half),
+            pltpu.VMEM((chunks, groups, ROWS, width), half),
+            pltpu.VMEM((chunks, groups, ROWS, width), half),
+            pltpu.VMEM((groups, chunks, ROWS, width + STAT), half),
+            pltpu.VMEM((chunks, groups, ROWS, width + STAT), half),
+            pltpu.VMEM((chunks, groups, ROWS, width + STAT), half),
+            pltpu.VMEM((groups, chunks, ROWS, width + STAT), half),
+            pltpu.VMEM((chunks, groups, 3, ROWS, width), half),
+            pltpu.VMEM((groups, chunks, 3, ROWS, width), half),
+            pltpu.VMEM((blocks, block_rows, width), full),
+            pltpu.VMEM((groups, chunks, ROWS, width), full),
+            pltpu.VMEM((groups, chunks, ROWS, STAT), full),
+            pltpu.VMEM((blocks * heads, block_rows, block_rows), full),
+            pltpu.VMEM((chunks * heads, block_rows, block_rows), full),
+            pltpu.VMEM((3, blocks, block_rows, width), full),
+            dma((2, planes, chunks)),
+            dma((planes, chunks)),
+            dma((9,)),
+            dma((9,)),
+            dma((3, groups)),
+            dma((3, groups)),
+            dma((chunks, groups)),
+            dma((chunks, groups)),
+            dma((chunks, groups)),
+            dma((chunks, groups)),
+            dma((chunks, groups)),
+            dma((chunks, groups)),
+        ],
+        compiler_params=pltpu.CompilerParams(
+            collective_id=0, has_side_effects=True, vmem_limit_bytes=56 << 20
+        ),
+    )(split(query_rows), split(key_rows), split(value_rows), split(out_grad), out_weight)
+    return tuple(result.reshape(tokens_here, width) for result in results)
+
+
+def fits(mesh):
+    return mesh.shape["seq"] == 8 and mesh.shape["head"] == 4
+
+
 def solution(mesh):
     placed = (
         P("seq", "head"),
@@ -251,7 +721,7 @@
         P("head", "seq"),
     )
     return jax.shard_map(
-        local,
+        fused_local if fits(mesh) else local,
         mesh=mesh,
         in_specs=placed,
         out_specs=(P("seq", "head"), P("seq", "head"), P("seq", "head"), P("seq", "head")),

time: 265 us -> 100 us (0.38)
  Pallas kernels: 0 us -> 94.4 us
  waiting for transfers between devices: 86.3 us -> 0 us
  local copies, waits for them, and re-layouts: 51.7 us -> 5.18 us
  starting transfers between devices: 37.9 us -> 0 us
  blocking collectives: 29.5 us -> 0 us
  matrix products: 25.2 us -> 0 us
  other arithmetic: 17.6 us -> 0 us
  between operations: 14.5 us -> 0.65 us
    pallas_call x0 -> x1, Pallas kernels: none -> 94.4 us  [fused_local(): pl.pallas_call(functools.partial(fused_kernel, groups, heads, chunks, pla...]
    all_gather x2 -> x0, waiting for transfers between devices: 58.6 us -> none  [the longest x1 37.9 us: local(): lax.all_gather(out_weight, 'seq', axis=1, tiled=True)]
    all_to_all x10 -> x0, starting transfers between devices: 37.9 us -> none  [the longest x1 4.33 us: local(): lax.all_to_all(far_grads[2].astype(jnp.bfloat16).reshape(groups, residues...]
    all_to_all x3 -> x0, blocking collectives: 29.5 us -> none  [the longest x1 12.1 us: local(): lax.all_to_all(group_view(query_rows), 'seq', split_axis=0, concat_axis=0...]
    all_to_all x10 -> x0, waiting for transfers between devices: 26.3 us -> none  [the longest x1 8.89 us: local(): lax.all_to_all(group_view(key_rows), 'seq', split_axis=0, concat_axis=0,...]
    dot_general x13 -> x0, matrix products: 25.2 us -> none  [the longest x1 6.62 us: local(): lax.dot_general(full_grad, lax.all_gather(out_weight, 'seq', axis=1, tile...]
    reshape x18 -> x0, local copies, waits for them, and re-layouts: 14.2 us -> none  [the longest x5 5.95 us: band_view(): return values.reshape(blocks_here, BLOCK, heads_here, DH)]
    convert_element_type x6 -> x0, other arithmetic: 9.65 us -> none  [the longest x1 2.62 us: local(): attended = ((band_factor[..., None] * out_band + far_factor[..., None] *...]
  transfers between devices with their start and end apart: 12 -> 0, of which waited for: 7 -> 0; matrix products, arithmetic and copies ran while one was open for 31% -> 0% of each run, Pallas kernels for 0% -> 0%
where the time goes in v1:
time: 100 us
  Pallas kernels  94.4 us (94%)
  local copies, waits for them, and re-layouts  5.18 us (5%)
    pallas_call x1, Pallas kernels, fused_local(): pl.pallas_call(functools.partial(fused_kernel, groups, heads, chunks, pla...  94.4 us
    unnamed x10, local copies, waits for them, and re-layouts  5.18 us

profile of v1, /device:TPU:0, one launch (start us, length us, event | category | flops | bytes accessed | tf_op | source)
XLA Modules:
  0.0 100.2 jit_solution(15069737205501302270)
XLA Ops:
  0.6 94.4 %shard_map.84 = (bf16[8,4,16,512]{3,2,1,0:T(8,128)(2,1)}, bf16[8,4,16,512]{3,2,1,0:T(8,128)(2,1)}, bf16[8,4,16,512]{3,2,1,0:T(8,128)(2,1)}, bf16[8,4,16,512]{3,2,1,0:T(8,128)(2,1)}) custom-call(bf16[8,4,16,512]{3,2,1,0:T(8,128)(2,1)} %bitcast.13, bf16[8,4,16,512]{3,2,1,0:T(8,128)(2,1)} %bitcast.14, bf16[8,4,16,512]{3,2,1,0:T(8,128)(2,1)} %bitcast.15, ...), custom_call_target="tpu_custom_call" | custom-call | tf_op jit(solution)/shard_map/pallas_call | solution.py:668
  95.0 0.0 copy-start.2
  95.0 1.9 %copy.13 = bf16[512,512]{1,0:T(8,128)(2,1)} copy(bf16[512,512]{1,0:T(8,128)(2,1)} %bitcast.12) | data formatting | bytes 1048576
  96.9 0.0 copy-done.2
  96.9 0.0 copy-start.1
  96.9 0.8 copy.14
  97.7 0.4 copy-done.1
  98.2 0.0 copy-start
  98.2 0.8 copy.15
  99.0 0.4 copy-done
  99.4 0.8 copy.16
Async XLA Ops:
  95.0 1.9 %copy-start.2 = (bf16[8,4,16,512]{3,2,1,0:T(8,128)(2,1)S(1)}, bf16[8,4,16,512]{3,2,1,0:T(8,128)(2,1)}, u32[]{:S(2)}) copy-start(bf16[8,4,16,512]{3,2,1,0:T(8,128)(2,1)} %get-tuple-element.9) | copy-start | bytes 1572868
  96.9 1.2 %copy-start.1 = (bf16[8,4,16,512]{3,2,1,0:T(8,128)(2,1)S(1)}, bf16[8,4,16,512]{3,2,1,0:T(8,128)(2,1)}, u32[]{:S(2)}) copy-start(bf16[8,4,16,512]{3,2,1,0:T(8,128)(2,1)} %get-tuple-element.10) | copy-start | bytes 1572868
  98.2 1.2 %copy-start = (bf16[8,4,16,512]{3,2,1,0:T(8,128)(2,1)S(1)}, bf16[8,4,16,512]{3,2,1,0:T(8,128)(2,1)}, u32[]{:S(2)}) copy-start(bf16[8,4,16,512]{3,2,1,0:T(8,128)(2,1)} %get-tuple-element.11) | copy-start | bytes 1572868

commit v2 on v1

--- a/solution.py
+++ b/solution.py
@@ -288,7 +288,7 @@
     q, k, v, og, w,
     att_out, dq_out, dk_out, dv_out,
     og_all, w_all, qf, kf, vf, g_home, gf, far_out, home_out, gr_send, gr_home,
-    out_band, att_full, lse_keep, s_band, s_far, band_grads,
+    out_band, att_full, lse_keep, s_band, s_far, band_grads, g_early,
     z_send, z_recv, w_send, w_recv, qkv_send, qkv_recv, out_send, out_recv,
     g_send, g_recv, gr_ssem, gr_rsem,
 ):
@@ -377,10 +377,6 @@
         ref = w_all.at[source, rows]
         return remote(ref, ref, w_send.at[index], w_recv.at[index], peer(o))
 
-    w_first = [w_own(0, 2), w_own(1, 4), w_own(2, 1)]
-    for copy in w_first:
-        copy.start()
-
     def qkv_copy(t, src, dst, o):
         return remote(src.at[other(o)], dst.at[:, s], qkv_send.at[t, o], qkv_recv.at[t, o], peer(o))
 
@@ -422,13 +418,8 @@
             kept = kept + place(lse, head, block_rows)
         lse_keep[pl.ds(2 * b, 2)] = kept.reshape(2, chunks, ROWS, STAT)
 
-    w_own(0, 2).wait_recv()
-    w_second = [w_part(3, other(2), low, 4), w_part(4, other(2), slice(None), 1)]
-    for copy in w_second:
-        copy.start()
-    w_own(1, 4).wait_recv()
-    w_third = [w_part(5, other(4), high, 2), w_part(6, other(4), slice(None), 1)]
-    for copy in w_third:
+    w_first = [w_own(0, 2), w_own(1, 4), w_own(2, 1)]
+    for copy in w_first:
         copy.start()
 
     def z_near(c):
@@ -437,23 +428,15 @@
             def _():
                 z_pass(slot, c)
 
-    def z_far(c):
-        for distance in range(2, planes):
-            for slot in range(planes):
-                @pl.when((h == slot + distance) | (h == slot - distance))
-                def _():
-                    z_pass(slot, c)
+    def z_far(c, distance):
+        for slot in range(planes):
+            @pl.when((h == slot + distance) | (h == slot - distance))
+            def _():
+                z_pass(slot, c)
 
     @pl.loop(0, chunks)
     def _(c):
         z_near(c)
-
-    w_part(3, other(6), low, 4).wait_recv()
-    w_fourth = [w_part(7, other(6), low, 1)]
-    w_fourth[0].start()
-    w_part(5, other(6), high, 2).wait_recv()
-    w_fourth.append(w_part(8, other(6), high, 1))
-    w_fourth[1].start()
 
     for o in range(1, groups):
         for t, (src, dst) in enumerate(triples):
@@ -483,17 +466,21 @@
             out_copy(c, o).start()
         home_out[s, c] = far_out[c, s]
 
-    @pl.loop(0, chunks)
-    def _(c):
-        @pl.when(inner)
-        def _():
-            z_far(c)
-
-    w_own(2, 1).wait_recv()
-    w_part(4, other(3), slice(None), 1).wait_recv()
-    w_part(6, other(5), slice(None), 1).wait_recv()
-    w_part(7, other(7), low, 1).wait_recv()
-    w_part(8, other(7), high, 1).wait_recv()
+    w_own(0, 2).wait_recv()
+    w_second = [w_part(3, other(2), low, 4), w_part(4, other(2), slice(None), 1)]
+    for copy in w_second:
+        copy.start()
+    w_own(1, 4).wait_recv()
+    w_third = [w_part(5, other(4), high, 2), w_part(6, other(4), slice(None), 1)]
+    for copy in w_third:
+        copy.start()
+
+    w_part(3, other(6), low, 4).wait_recv()
+    w_fourth = [w_part(7, other(6), low, 1)]
+    w_fourth[0].start()
+    w_part(5, other(6), high, 2).wait_recv()
+    w_fourth.append(w_part(8, other(6), high, 1))
+    w_fourth[1].start()
 
     @pl.loop(0, chunks)
     def _(c):
@@ -536,16 +523,46 @@
     def _(c):
         og_all[h, c] = og[:, c]
 
+    per = og.shape[-1] // w.shape[1]
+    depth = w.shape[1]
+    first = h // 2
+    last = (planes - 1) * (1 - first)
+
+    @pl.when(inner)
+    def _():
+        for c in range(2):
+            z_far(c, 2)
+
+    @pl.when(jnp.logical_not(inner))
+    def _():
+        for c in range(chunks):
+            z_far(c, 2)
+
+    w_own(2, 1).wait_recv()
+    w_part(4, other(3), slice(None), 1).wait_recv()
+    w_part(6, other(5), slice(None), 1).wait_recv()
+    w_part(7, other(7), low, 1).wait_recv()
+    w_part(8, other(7), high, 1).wait_recv()
+
+    early = jnp.zeros((chunks * block_rows, width), jnp.float32)
+    for slot in range(planes - 1):
+        for part in range(per):
+            left = og_all[first + slot, :, :, :, part * depth:(part + 1) * depth]
+            early = early + dot_nt(left.reshape(chunks * block_rows, depth), w_all[(first + slot) * per + part])
+    g_early[...] = early.reshape(chunks, block_rows, width)
+
     def grad_chunk(c):
+        @pl.when(inner & (c < chunks - 2))
+        def _():
+            z_far(c + 2, 2)
+
         @pl.when(jnp.logical_not(inner))
         def _():
-            z_far(c)
-        total = jnp.zeros((block_rows, width), jnp.float32)
-        depth = w.shape[1]
-        for source in range(groups):
-            per = og.shape[-1] // depth
-            left = og_all[source // per, c, :, :, (source % per) * depth:(source % per + 1) * depth]
-            total = total + dot_nt(left.reshape(block_rows, depth), w_all[source])
+            z_far(c, planes - 1)
+        total = g_early[c]
+        for part in range(per):
+            left = og_all[last, c, :, :, part * depth:(part + 1) * depth]
+            total = total + dot_nt(left.reshape(block_rows, depth), w_all[last * per + part])
         grad = total.astype(jnp.bfloat16)
         g_home[:, c, :, :width] = grad.reshape(groups, ROWS, width)
         grad = grad.astype(jnp.float32)
@@ -688,6 +705,7 @@
             pltpu.VMEM((blocks * heads, block_rows, block_rows), full),
             pltpu.VMEM((chunks * heads, block_rows, block_rows), full),
             pltpu.VMEM((3, blocks, block_rows, width), full),
+            pltpu.VMEM((chunks, block_rows, width), full),
             dma((2, planes, chunks)),
             dma((planes, chunks)),
             dma((9,)),

time: 100 us -> 100 us (level)
  no operation moved by 1% of the time
where the time goes in v2:
time: 100 us
  Pallas kernels  94.2 us (94%)
  local copies, waits for them, and re-layouts  5.18 us (5%)
    pallas_call x1, Pallas kernels, fused_local(): pl.pallas_call(functools.partial(fused_kernel, groups, heads, chunks, pla...  94.2 us
    unnamed x10, local copies, waits for them, and re-layouts  5.18 us

profile of v2, /device:TPU:0, one launch (start us, length us, event | category | flops | bytes accessed | tf_op | source)
XLA Modules:
  0.0 100.1 jit_solution(9177476370202838740)
XLA Ops:
  0.6 94.2 %shard_map.84 = (bf16[8,4,16,512]{3,2,1,0:T(8,128)(2,1)}, bf16[8,4,16,512]{3,2,1,0:T(8,128)(2,1)}, bf16[8,4,16,512]{3,2,1,0:T(8,128)(2,1)}, bf16[8,4,16,512]{3,2,1,0:T(8,128)(2,1)}) custom-call(bf16[8,4,16,512]{3,2,1,0:T(8,128)(2,1)} %bitcast.13, bf16[8,4,16,512]{3,2,1,0:T(8,128)(2,1)} %bitcast.14, bf16[8,4,16,512]{3,2,1,0:T(8,128)(2,1)} %bitcast.15, ...), custom_call_target="tpu_custom_call" | custom-call | tf_op jit(solution)/shard_map/pallas_call | solution.py:685
  94.9 0.0 copy-start.2
  94.9 1.9 %copy.13 = bf16[512,512]{1,0:T(8,128)(2,1)} copy(bf16[512,512]{1,0:T(8,128)(2,1)} %bitcast.12) | data formatting | bytes 1048576
  96.8 0.0 copy-done.2
  96.8 0.0 copy-start.1
  96.8 0.8 copy.14
  97.6 0.4 copy-done.1
  98.0 0.0 copy-start
  98.0 0.8 copy.15
  98.8 0.4 copy-done
  99.3 0.8 copy.16
Async XLA Ops:
  94.9 1.9 %copy-start.2 = (bf16[8,4,16,512]{3,2,1,0:T(8,128)(2,1)S(1)}, bf16[8,4,16,512]{3,2,1,0:T(8,128)(2,1)}, u32[]{:S(2)}) copy-start(bf16[8,4,16,512]{3,2,1,0:T(8,128)(2,1)} %get-tuple-element.9) | copy-start | bytes 1572868
  96.8 1.2 %copy-start.1 = (bf16[8,4,16,512]{3,2,1,0:T(8,128)(2,1)S(1)}, bf16[8,4,16,512]{3,2,1,0:T(8,128)(2,1)}, u32[]{:S(2)}) copy-start(bf16[8,4,16,512]{3,2,1,0:T(8,128)(2,1)} %get-tuple-element.10) | copy-start | bytes 1572868
  98.0 1.2 %copy-start = (bf16[8,4,16,512]{3,2,1,0:T(8,128)(2,1)S(1)}, bf16[8,4,16,512]{3,2,1,0:T(8,128)(2,1)}, u32[]{:S(2)}) copy-start(bf16[8,4,16,512]{3,2,1,0:T(8,128)(2,1)} %get-tuple-element.11) | copy-start | bytes 1572868

commit v3 on v2

--- a/solution.py
+++ b/solution.py
@@ -482,6 +482,11 @@
     w_fourth.append(w_part(8, other(6), high, 1))
     w_fourth[1].start()
 
+    @pl.when(inner)
+    def _():
+        for c in range(2):
+            z_far(c, 2)
+
     @pl.loop(0, chunks)
     def _(c):
         for o in range(1, groups):
@@ -528,11 +533,6 @@
     first = h // 2
     last = (planes - 1) * (1 - first)
 
-    @pl.when(inner)
-    def _():
-        for c in range(2):
-            z_far(c, 2)
-
     @pl.when(jnp.logical_not(inner))
     def _():
         for c in range(chunks):
@@ -664,6 +664,17 @@
             @pl.when((h < slot) & (h > 0))
             def _():
                 z_copy(slot, c, 1).wait_send()
+
+
+def settle_kernel(a, b, c, d, a_out, b_out, c_out, d_out, sems):
+    copies = [
+        pltpu.make_async_copy(source, target, sems.at[index])
+        for index, (source, target) in enumerate(((a, a_out), (b, b_out), (c, c_out), (d, d_out)))
+    ]
+    for copy in copies:
+        copy.start()
+    for copy in copies:
+        copy.wait()
 
 
 def fused_local(query_rows, key_rows, value_rows, out_grad, out_weight):
@@ -723,6 +734,14 @@
             collective_id=0, has_side_effects=True, vmem_limit_bytes=56 << 20
         ),
     )(split(query_rows), split(key_rows), split(value_rows), split(out_grad), out_weight)
+    anywhere = pl.BlockSpec(memory_space=pl.ANY)
+    results = pl.pallas_call(
+        settle_kernel,
+        out_shape=[jax.ShapeDtypeStruct(result.shape, half) for result in results],
+        in_specs=[in_vmem] * 4,
+        out_specs=[anywhere] * 4,
+        scratch_shapes=[dma((4,))],
+    )(*results)
     return tuple(result.reshape(tokens_here, width) for result in results)
 
 

time: 100 us -> 97.1 us (0.971)
  local copies, waits for them, and re-layouts: 5.18 us -> 0 us
  Pallas kernels: 94.2 us -> 96.3 us
    unnamed x10 -> x0, local copies, waits for them, and re-layouts: 5.18 us -> none
    pallas_call x0 -> x1, Pallas kernels: none -> 2.86 us  [fused_local(): pl.pallas_call(settle_kernel, out_shape=[jax.ShapeDtypeStruct(result.shap...]
where the time goes in v3:
time: 97.1 us; the launch traced here: 96.9 us
  Pallas kernels  96.3 us (99%)
    pallas_call x1, Pallas kernels, fused_local(): pl.pallas_call(functools.partial(fused_kernel, groups, heads, chunks, pla...  93.4 us
    pallas_call x1, Pallas kernels, fused_local(): pl.pallas_call(settle_kernel, out_shape=[jax.ShapeDtypeStruct(result.shap...  2.86 us

profile of v3, /device:TPU:0, one launch (start us, length us, event | category | flops | bytes accessed | tf_op | source)
XLA Modules:
  0.0 96.9 jit_solution(2881592484243728543)
XLA Ops:
  0.6 93.4 %shard_map.84 = (bf16[8,4,16,512]{3,2,1,0:T(8,128)(2,1)}, bf16[8,4,16,512]{3,2,1,0:T(8,128)(2,1)}, bf16[8,4,16,512]{3,2,1,0:T(8,128)(2,1)}, bf16[8,4,16,512]{3,2,1,0:T(8,128)(2,1)}) custom-call(bf16[8,4,16,512]{3,2,1,0:T(8,128)(2,1)} %bitcast.9, bf16[8,4,16,512]{3,2,1,0:T(8,128)(2,1)} %bitcast.10, bf16[8,4,16,512]{3,2,1,0:T(8,128)(2,1)} %bitcast.11, ...), custom_call_target="tpu_custom_call" | custom-call | tf_op jit(solution)/shard_map/pallas_call | solution.py:696
  94.0 2.9 %shard_map.85 = (bf16[8,4,16,512]{3,2,1,0:T(8,128)(2,1)}, bf16[8,4,16,512]{3,2,1,0:T(8,128)(2,1)}, bf16[8,4,16,512]{3,2,1,0:T(8,128)(2,1)}, bf16[8,4,16,512]{3,2,1,0:T(8,128)(2,1)}) custom-call(bf16[8,4,16,512]{3,2,1,0:T(8,128)(2,1)} %get-tuple-element.12.a, bf16[8,4,16,512]{3,2,1,0:T(8,128)(2,1)} %get-tuple-element.13.b, ...), custom_call_target="tpu_custom_call" | custom-call | tf_op jit(solution)/shard_map/pallas_call | solution.py:738
